TPU v7x, 512 devices: a whole 4x4x16 slice. The times are simulated.
512 devices in a mesh: row: 16 (over z_lo, core), col: 32 (over y, x, z_hi).
Axes of the slice: x: 4, y: 4, z: 16 (z_hi: 2, z_lo: 8; z = z_hi * 8 + z_lo), core: 2. Of those that a mesh axis runs over, the one named last changes fastest.
Arguments:
- signatures: bfloat16 [8192, 49152], P('row', 'col'), as said below
- trailing: float32 [8192, 4096], P('row', 'col'), may hold values from -6 to 6
- ridge: float32 [1], replicated, may hold values from 0.5 to 2
- panel_index: int32 [1], replicated, may hold values from 1 to 15
Outputs:
- factor: float32 [8192, 256], P(('row', 'col'))
- updated: float32 [8192, 4096], P('row', 'col')
Inputs may be any that keep to these rules, and one draw needn't show every extreme that they name: `signatures`: every diagonal block of the Gram matrix plus the ridge is positive definite.
All inputs are finite; a program needn't handle non-finite values.
Results may differ from a plain program's by a relative error of at most 0.0003.
Values may be sent and summed in bfloat16 or wider, within the bound.
No kernel may reach another device: no remote copies, remote signals or barrier semaphores. Data moves between devices by JAX's collectives and lax.ppermute only.
A program may use at most 64 MiB of HBM per device.

v0:
```python
import jax
import jax.numpy as jnp
from jax import lax
from jax.sharding import PartitionSpec as P

PANEL = 256


def spread(block, axis, owner):
    block = jnp.where(lax.axis_index(axis) == owner, block, jnp.zeros_like(block))
    return lax.psum(block, axis)


def add_ridge(block, first_row, panel_start, ridge):
    row_ids = first_row + lax.broadcasted_iota(jnp.int32, block.shape, 0)
    col_ids = panel_start + lax.broadcasted_iota(jnp.int32, block.shape, 1)
    return block + jnp.where(row_ids == col_ids, ridge[0], jnp.zeros((), block.dtype))


def mask_above(block, first_row, panel_start):
    row_ids = first_row + lax.broadcasted_iota(jnp.int32, block.shape, 0)
    return jnp.where(row_ids >= panel_start, block, jnp.zeros((), block.dtype))


def solve_rows(lower, panel_rows):
    return jax.scipy.linalg.solve_triangular(lower, panel_rows.T, lower=True).T


def local(signatures, trailing, ridge, panel_index):
    rows_dev = signatures.shape[0]
    tile_cols = trailing.shape[1]
    col_count = lax.axis_size("col")
    row_share = rows_dev // col_count
    row_pos = lax.axis_index("row")
    col_pos = lax.axis_index("col")
    panel_start = panel_index[0] * PANEL
    row_owner = panel_start // rows_dev
    local_offset = panel_start % rows_dev
    own_paths = lax.dynamic_slice_in_dim(signatures, local_offset, PANEL, 0)
    panel_paths = spread(own_paths, "row", row_owner)
    mine_rows = lax.psum_scatter(
        lax.dot_general(
            signatures, panel_paths, (((1,), (1,)), ((), ())), preferred_element_type=jnp.float32
        ),
        "col",
        scatter_dimension=0,
        tiled=True,
    )
    mine_rows = add_ridge(mine_rows, row_pos * rows_dev + col_pos * row_share, panel_start, ridge)
    source_rows = lax.all_gather(mine_rows, "col", axis=0, tiled=True)
    block_cut = lax.dynamic_slice_in_dim(source_rows, local_offset, PANEL, 0)
    diagonal = spread(block_cut, "row", row_owner)
    lower = jnp.linalg.cholesky(diagonal)
    factor_mine = solve_rows(lower, mine_rows)
    factor_mine = mask_above(factor_mine, row_pos * rows_dev + col_pos * row_share, panel_start)
    factor_block = lax.all_gather(factor_mine, "col", axis=0, tiled=True)
    window_start = panel_start + PANEL + col_pos * tile_cols
    window_owner = window_start // rows_dev
    window_cut = lax.dynamic_slice_in_dim(factor_block, window_start % rows_dev, tile_cols, 0)
    window_rows = spread(window_cut, "row", window_owner)
    updated = trailing - lax.dot_general(
        factor_block,
        window_rows,
        (((1,), (1,)), ((), ())),
        precision=lax.Precision.HIGHEST,
        preferred_element_type=jnp.float32,
    )
    return (factor_mine, updated)


def solution(mesh):
    placed = (P("row", "col"), P("row", "col"), P(), P())
    return jax.shard_map(
        local,
        mesh=mesh,
        in_specs=placed,
        out_specs=(P(("row", "col"), None), P("row", "col")),
        check_vma=False,
    )
```

profile of v0, /device:TPU:1, one launch (start us, length us, event | category | flops | bytes accessed | tf_op | source)
XLA Modules:
  0.0 1291.1 jit_solution(10216238595232170383)
XLA Ops:
  8.0 2.3 dynamic-slice_select_fusion
  10.4 204.1 %all-reduce.5.cloned.1.call-done = bf16[256,1536]{1,0:T(8,128)(2,1)} async-done(((bf16[256,1536]{1,0:T(8,128)(2,1)}), bf16[256,1536]{1,0:T(8,128)(2,1)}) %all-reduce.5.cloned.1.call-update) | async-done | bytes 786448 | tf_op jit(solution)/shard_map/psum | solution.py:11
  214.4 1.7 convolution_bitcast_fusion
  216.2 1.0 copy.18
  217.9 283.6 %reduce-scatter.4.cloned.1.call-done = f32[16,256]{1,0:T(8,128)} async-done(((f32[512,256]{1,0:T(8,128)}), f32[16,256]{1,0:T(8,128)}) %reduce-scatter.4.cloned.1.call-update) | async-done | bytes 16400
  501.6 0.8 copy.19
  502.5 137.0 %all_gather.6 = f32[512,256]{1,0:T(8,128)S(1)} all-gather(f32[16,256]{1,0:T(8,128)S(1)} %copy.11), channel_id=1, replica_groups=mesh['row'=16,'col'=32] {'col'}, dimensions={0}, use_global_device_ids=true | all-gather | bytes 540672 | tf_op jit(solution)/shard_map/all_gather | solution.py:50
  639.7 0.7 broadcast_select_fusion
  640.7 231.9 %all-reduce.7.cloned.1.call-done = f32[256,256]{0,1:T(8,128)} async-done(((f32[256,256]{0,1:T(8,128)}), f32[256,256]{0,1:T(8,128)}) %all-reduce.7.cloned.1.call-update) | async-done | bytes 262160 | tf_op jit(solution)/shard_map/psum | solution.py:11
  872.6 1.1 copy.13
  873.7 1.0 fusion
  874.7 11.7 cholesky.49
  886.4 9.8 custom-call.15
  896.7 11.7 cholesky.103
  908.8 0.6 compare_reduce_fusion
  910.9 4.4 while.1
  911.1 0.6 fusion.20
  911.6 1.4 dynamic-slice.7
  913.8 1.4 dynamic-slice.7
  915.3 19.7 %custom-call.16 = f32[2,128,128]{1,2,0:T(8,128)S(1)} custom-call(f32[2,128,128]{2,1,0:T(8,128)S(1)} %get-tuple-element.9), custom_call_target="InvertDiagBlocksLowerTriangular" | custom-call | tf_op jit(solution)/shard_map/jit(_solve_triangular)/triangular_solve | solution.py:26
  935.8 145.4 %all_gather.7 = f32[512,256]{1,0:T(8,128)S(1)} all-gather(f32[16,256]{1,0:T(8,128)S(1)} %fusion.8), channel_id=1, replica_groups=mesh['row'=16,'col'=32] {'col'}, dimensions={0}, use_global_device_ids=true | all-gather | bytes 540672 | tf_op jit(solution)/shard_map/all_gather | solution.py:56
  1081.2 0.7 dynamic-slice_select_fusion.1
  1081.9 200.4 %all-reduce.9.cloned.1.call-done = f32[128,256]{1,0:T(8,128)} async-done(((f32[128,256]{1,0:T(8,128)}), f32[128,256]{1,0:T(8,128)}) %all-reduce.9.cloned.1.call-update) | async-done | bytes 131088 | tf_op jit(solution)/shard_map/psum | solution.py:11
  1282.4 2.2 convolution_subtract_fusion
  (48 shorter events, 3.3 us)
Async XLA Ops:
  7.2 207.3 %copy-start = (bf16[512,1536]{1,0:T(8,128)(2,1)S(1)}, bf16[512,1536]{1,0:T(8,128)(2,1)}, u32[]{:S(2)}) copy-start(bf16[512,1536]{1,0:T(8,128)(2,1)} %param.4) | copy-start | bytes 4718596
  7.2 207.3 %all-reduce.5.cloned.1.call-start = ((), (), s32[]{:S(2)}) async-start(), calls=%async_computation.1 | async-start | bytes 1572864 | tf_op jit(solution)/shard_map/psum | solution.py:11
  10.3 491.2 %reduce-scatter.4.cloned.1.call-start = ((), (), s32[]{:S(2)}) async-start(), calls=%async_computation.4 | async-start | bytes 540672
  217.2 655.4 %all-reduce.7.cloned.1.call-start = ((), (), s32[]{:S(2)}) async-start(), calls=%async_computation.2 | async-start | bytes 524288 | tf_op jit(solution)/shard_map/psum | solution.py:11
  640.5 641.9 %all-reduce.9.cloned.1.call-start = ((), (), s32[]{:S(2)}) async-start(), calls=%async_computation.3 | async-start | bytes 262144 | tf_op jit(solution)/shard_map/psum | solution.py:11
  910.9 371.5 %copy-start.1 = (f32[512,128]{1,0:T(8,128)S(1)}, f32[512,128]{1,0:T(8,128)}, u32[]{:S(2)}) copy-start(f32[512,128]{1,0:T(8,128)} %param.5) | copy-start | bytes 786436
  935.8 348.7 %copy-start.2 = (f32[16,256]{1,0:T(8,128)}, f32[16,256]{1,0:T(8,128)S(1)}, u32[]{:S(2)}) copy-start(f32[16,256]{1,0:T(8,128)S(1)} %fusion.8) | copy-start | bytes 49156
Sparse Core Ops, SparseCore 0:
  10.9 203.4 all-reduce.4
  217.5 284.0 reduce-scatter.3
  640.6 231.9 all-reduce.6
  1082.0 200.2 all-reduce.8
where the time goes:
time: 1290 us
  waiting for transfers between devices  920 us (71%)
  blocking collectives  282 us (22%)
  other arithmetic  58.6 us (5%)
  between operations  16.8 us (1%)
    psum x3, waiting for transfers between devices, spread(): return lax.psum(block, axis)  636 us
    unnamed x5, waiting for transfers between devices  284 us
    all_gather x1, blocking collectives, local(): factor_block = lax.all_gather(factor_mine, 'col', axis=0, tiled=True)  145 us
    all_gather x1, blocking collectives, local(): source_rows = lax.all_gather(mine_rows, 'col', axis=0, tiled=True)  137 us
    another operation x6, other arithmetic, local(): lower = jnp.linalg.cholesky(diagonal)  34 us
  transfers between devices with their start and end apart: 4, of which 4 were waited for; matrix products, arithmetic and copies ran while one was open for 0% of the time, Pallas kernels for 0%

commit v1 on v0

--- a/solution.py
+++ b/solution.py
@@ -4,6 +4,10 @@
 from jax.sharding import PartitionSpec as P
 
 PANEL = 256
+strips_all_extend = lambda local_x: jnp.concatenate(
+    lax.all_to_all(jnp.stack([local_x for _ in range(lax.axis_size("col"))], axis=0), "col", 0, 0),
+    axis=0,
+)
 
 
 def spread(block, axis, owner):
@@ -53,7 +57,7 @@
     lower = jnp.linalg.cholesky(diagonal)
     factor_mine = solve_rows(lower, mine_rows)
     factor_mine = mask_above(factor_mine, row_pos * rows_dev + col_pos * row_share, panel_start)
-    factor_block = lax.all_gather(factor_mine, "col", axis=0, tiled=True)
+    factor_block = strips_all_extend(factor_mine)
     window_start = panel_start + PANEL + col_pos * tile_cols
     window_owner = window_start // rows_dev
     window_cut = lax.dynamic_slice_in_dim(factor_block, window_start % rows_dev, tile_cols, 0)

time: 1290 us -> 1170 us (0.907)
  blocking collectives: 282 us -> 137 us
    all_gather x1 -> x0, blocking collectives: 145 us -> none  [local(): factor_block = lax.all_gather(factor_mine, 'col', axis=0, tiled=True)]
    all_to_all x0 -> x1, waiting for transfers between devices: none -> 20.4 us  [lax.all_to_all(jnp.stack([local_x for _ in range(lax.axis_size('col'))],...]
  transfers between devices with their start and end apart: 4 -> 5, of which waited for: 4 -> 5; matrix products, arithmetic and copies ran while one was open for 0% -> 0% of each run, Pallas kernels for 0% -> 0%
where the time goes in v1:
time: 1170 us
  waiting for transfers between devices  931 us (80%)
  blocking collectives  137 us (12%)
  other arithmetic  58.6 us (5%)
  between operations  16.8 us (1%)
    psum x3, waiting for transfers between devices, spread(): return lax.psum(block, axis)  627 us
    unnamed x5, waiting for transfers between devices  284 us
    all_gather x1, blocking collectives, local(): source_rows = lax.all_gather(mine_rows, 'col', axis=0, tiled=True)  137 us
    another operation x6, other arithmetic, local(): lower = jnp.linalg.cholesky(diagonal)  34 us
  transfers between devices with their start and end apart: 5, of which 5 were waited for; matrix products, arithmetic and copies ran while one was open for 0% of the time, Pallas kernels for 0%

profile of v1, /device:TPU:1, one launch (start us, length us, event | category | flops | bytes accessed | tf_op | source)
XLA Modules:
  0.0 1167.5 jit_solution(8469010676368935692)
XLA Ops:
  8.0 2.3 dynamic-slice_select_fusion
  10.4 204.1 %all-reduce.5.cloned.1.call-done = bf16[256,1536]{1,0:T(8,128)(2,1)} async-done(((bf16[256,1536]{1,0:T(8,128)(2,1)}), bf16[256,1536]{1,0:T(8,128)(2,1)}) %all-reduce.5.cloned.1.call-update) | async-done | bytes 786448 | tf_op jit(solution)/shard_map/psum | solution.py:15
  214.4 1.7 convolution_bitcast_fusion
  216.2 1.0 copy.18
  217.9 283.6 %reduce-scatter.4.cloned.1.call-done = f32[16,256]{1,0:T(8,128)} async-done(((f32[512,256]{1,0:T(8,128)}), f32[16,256]{1,0:T(8,128)}) %reduce-scatter.4.cloned.1.call-update) | async-done | bytes 16400
  501.6 0.8 copy.19
  502.5 137.0 %all_gather.3 = f32[512,256]{1,0:T(8,128)S(1)} all-gather(f32[16,256]{1,0:T(8,128)S(1)} %copy.11), channel_id=1, replica_groups=mesh['row'=16,'col'=32] {'col'}, dimensions={0}, use_global_device_ids=true | all-gather | bytes 540672 | tf_op jit(solution)/shard_map/all_gather | solution.py:54
  639.7 0.7 broadcast_select_fusion
  640.6 232.0 %all-reduce.7.cloned.1.call-done = f32[256,256]{0,1:T(8,128)} async-done(((f32[256,256]{0,1:T(8,128)}), f32[256,256]{0,1:T(8,128)}) %all-reduce.7.cloned.1.call-update) | async-done | bytes 262160 | tf_op jit(solution)/shard_map/psum | solution.py:15
  872.6 1.1 copy.13
  873.7 1.0 fusion
  874.7 11.7 %cholesky.49 = f32[128,128]{1,0:T(8,128)S(1)} custom-call(f32[128,128]{1,0:T(8,128)S(1)} %cholesky.115), custom_call_target="Cholesky" | custom-call | tf_op jit(solution)/shard_map/jit(cholesky)/cholesky | solution.py:57
  886.4 9.8 custom-call.15
  896.7 11.7 %cholesky.103 = f32[128,128]{1,0:T(8,128)S(1)} custom-call(f32[128,128]{1,0:T(8,128)S(1)} %convolution_subtract_fusion.2), custom_call_target="Cholesky" | custom-call | tf_op jit(solution)/shard_map/jit(cholesky)/cholesky | solution.py:57
  910.9 4.4 while.1
  911.6 1.4 dynamic-slice.7
  913.7 1.4 dynamic-slice.7
  915.3 19.7 %custom-call.16 = f32[2,128,128]{1,2,0:T(8,128)S(1)} custom-call(f32[2,128,128]{2,1,0:T(8,128)S(1)} %get-tuple-element.9), custom_call_target="InvertDiagBlocksLowerTriangular" | custom-call | tf_op jit(solution)/shard_map/jit(_solve_triangular)/triangular_solve | solution.py:30
  935.8 0.9 stack.2
  936.7 9.7 all-to-all-start
  946.5 20.4 %all-to-all-done = f32[32,16,256]{2,1,0:T(8,128)S(1)} async-done(((f32[32,16,256]{2,1,0:T(8,128)}), f32[32,16,256]{2,1,0:T(8,128)S(1)}, u32[]{:S(2)}, u32[]{:S(2)}) %all-to-all-start) | async-done | bytes 524320 | tf_op jit(solution)/shard_map/all_to_all | solution.py:8
  966.9 0.7 dynamic-slice_select_fusion.1
  967.6 191.2 %all-reduce.9.cloned.1.call-done = f32[128,256]{1,0:T(8,128)} async-done(((f32[128,256]{1,0:T(8,128)}), f32[128,256]{1,0:T(8,128)}) %all-reduce.9.cloned.1.call-update) | async-done | bytes 131088 | tf_op jit(solution)/shard_map/psum | solution.py:15
  1158.8 2.2 convolution_subtract_fusion
  (50 shorter events, 4.5 us)
Async XLA Ops:
  7.2 207.3 %copy-start = (bf16[512,1536]{1,0:T(8,128)(2,1)S(1)}, bf16[512,1536]{1,0:T(8,128)(2,1)}, u32[]{:S(2)}) copy-start(bf16[512,1536]{1,0:T(8,128)(2,1)} %param.4) | copy-start | bytes 4718596
  7.2 207.3 %all-reduce.5.cloned.1.call-start = ((), (), s32[]{:S(2)}) async-start(), calls=%async_computation.2 | async-start | bytes 1572864 | tf_op jit(solution)/shard_map/psum | solution.py:15
  10.3 491.2 %reduce-scatter.4.cloned.1.call-start = ((), (), s32[]{:S(2)}) async-start(), calls=%async_computation.5 | async-start | bytes 540672
  217.2 655.4 %all-reduce.7.cloned.1.call-start = ((), (), s32[]{:S(2)}) async-start(), calls=%async_computation.3 | async-start | bytes 524288 | tf_op jit(solution)/shard_map/psum | solution.py:15
  915.3 243.5 %copy-start.1 = (f32[512,128]{1,0:T(8,128)S(1)}, f32[512,128]{1,0:T(8,128)}, u32[]{:S(2)}) copy-start(f32[512,128]{1,0:T(8,128)} %param.5) | copy-start | bytes 786436
  935.8 225.1 %copy-start.2 = (f32[16,256]{1,0:T(8,128)}, f32[16,256]{1,0:T(8,128)S(1)}, u32[]{:S(2)}) copy-start(f32[16,256]{1,0:T(8,128)S(1)} %fusion.8) | copy-start | bytes 49156
  936.7 30.2 %all-to-all-start = ((f32[32,16,256]{2,1,0:T(8,128)}), f32[32,16,256]{2,1,0:T(8,128)S(1)}, u32[]{:S(2)}, u32[]{:S(2)}) async-start(f32[32,16,256]{2,1,0:T(8,128)} %stack.2), calls=%async_computation | async-start | bytes 1048576 | tf_op jit(solution)/shard_map/all_to_all | solution.py:8
  946.4 212.4 %all-reduce.9.cloned.1.call-start = ((), (), s32[]{:S(2)}) async-start(), calls=%async_computation.4 | async-start | bytes 262144 | tf_op jit(solution)/shard_map/psum | solution.py:15
Sparse Core Ops, SparseCore 0:
  10.9 203.4 all-reduce.4
  217.5 284.0 reduce-scatter.3
  640.6 231.9 all-reduce.6
  967.7 191.0 all-reduce.8

commit v2 on v0

--- a/solution.py
+++ b/solution.py
@@ -8,7 +8,12 @@
 
 def spread(block, axis, owner):
     block = jnp.where(lax.axis_index(axis) == owner, block, jnp.zeros_like(block))
-    return lax.psum(block, axis)
+
+    def find_the_results(body, dev_axis):
+        right_arr = jnp.sum(jax.lax.all_gather(body, dev_axis), 0)
+        return right_arr
+
+    return find_the_results(block, axis)
 
 
 def add_ridge(block, first_row, panel_start, ridge):

time: 1290 us -> 1060 us (0.82)
  waiting for transfers between devices: 920 us -> 685 us
    psum x3 -> x0, waiting for transfers between devices: 636 us -> none  [spread(): return lax.psum(block, axis)]
    all_gather x0 -> x3, waiting for transfers between devices: none -> 401 us  [find_the_results(): right_arr = jnp.sum(jax.lax.all_gather(body, dev_axis), 0)]
    unnamed x5 -> x4, waiting for transfers between devices: 284 us -> 0.07 us
    reduce_scatter x0 -> x1, waiting for transfers between devices: none -> 283 us  [local(): lax.psum_scatter(lax.dot_general(signatures, panel_paths, (((1,), (1,)),...]
where the time goes in v2:
time: 1060 us
  waiting for transfers between devices  685 us (65%)
  blocking collectives  280 us (26%)
  other arithmetic  70.2 us (7%)
  between operations  16.6 us (2%)
    all_gather x3, waiting for transfers between devices, find_the_results(): right_arr = jnp.sum(jax.lax.all_gather(body, dev_axis), 0)  401 us
    reduce_scatter x1, waiting for transfers between devices, local(): lax.psum_scatter(lax.dot_general(signatures, panel_paths, (((1,), (1,)),...  283 us
    all_gather x1, blocking collectives, local(): factor_block = lax.all_gather(factor_mine, 'col', axis=0, tiled=True)  144 us
    all_gather x1, blocking collectives, local(): source_rows = lax.all_gather(mine_rows, 'col', axis=0, tiled=True)  136 us
    another operation x6, other arithmetic, local(): lower = jnp.linalg.cholesky(diagonal)  34 us
  transfers between devices with their start and end apart: 4, of which 4 were waited for; matrix products, arithmetic and copies ran while one was open for 0% of the time, Pallas kernels for 0%

profile of v2, /device:TPU:1, one launch (start us, length us, event | category | flops | bytes accessed | tf_op | source)
XLA Modules:
  0.0 1060.0 jit_solution(6581669432801921725)
XLA Ops:
  7.9 2.3 dynamic-slice_select_fusion
  10.3 151.2 %all-gather.7.cloned.1.call-done = bf16[4096,1536]{1,0:T(8,128)(2,1)} async-done(((bf16[256,1536]{1,0:T(8,128)(2,1)}), bf16[4096,1536]{1,0:T(8,128)(2,1)}) %all-gather.7.cloned.1.call-update) | async-done | bytes 12582928 | tf_op jit(solution)/shard_map/all_gather | solution.py:13
  161.4 6.9 reduce_sum.30
  168.3 1.4 convolution_bitcast_fusion
  170.5 283.4 %reduce-scatter.2.cloned.1.call-done = f32[16,256]{1,0:T(8,128)} async-done(((f32[512,256]{1,0:T(8,128)}), f32[16,256]{1,0:T(8,128)}) %reduce-scatter.2.cloned.1.call-update) | async-done | bytes 16400 | tf_op jit(solution)/shard_map/reduce_scatter | solution.py:46
  453.8 0.8 select_add_fusion
  454.6 135.6 %all_gather.26 = f32[512,256]{1,0:T(8,128)S(1)} all-gather(f32[16,256]{1,0:T(8,128)S(1)} %select_add_fusion), channel_id=1, replica_groups=mesh['row'=16,'col'=32] {'col'}, dimensions={0}, use_global_device_ids=true | all-gather | bytes 540672 | tf_op jit(solution)/shard_map/all_gather | solution.py:55
  590.3 0.7 dynamic-slice_select_fusion.1
  591.3 0.8 fusion.18
  592.1 143.0 %all-gather.9.cloned.1.call-done = f32[4096,256]{1,0:T(8,128)} async-done(((f32[256,256]{1,0:T(8,128)}), f32[4096,256]{1,0:T(8,128)}) %all-gather.9.cloned.1.call-update) | async-done | bytes 4194320 | tf_op jit(solution)/shard_map/all_gather | solution.py:13
  735.1 2.5 reduce_sum.31
  737.8 11.7 %cholesky.49 = f32[128,128]{1,0:T(8,128)S(1)} custom-call(f32[128,128]{1,0:T(8,128)S(1)} %cholesky.115), custom_call_target="Cholesky" | custom-call | tf_op jit(solution)/shard_map/jit(cholesky)/cholesky | solution.py:58
  749.5 9.8 custom-call.15
  759.8 11.7 %cholesky.103 = f32[128,128]{1,0:T(8,128)S(1)} custom-call(f32[128,128]{1,0:T(8,128)S(1)} %convolution_subtract_fusion.1), custom_call_target="Cholesky" | custom-call | tf_op jit(solution)/shard_map/jit(cholesky)/cholesky | solution.py:58
  771.6 0.7 compare_reduce_fusion
  773.8 4.3 while.1
  774.5 1.4 bitcast_dynamic-update-slice_fusion.2
  776.6 1.4 bitcast_dynamic-update-slice_fusion.2
  778.0 19.7 %custom-call.16 = f32[2,128,128]{1,2,0:T(8,128)S(1)} custom-call(f32[2,128,128]{2,1,0:T(8,128)S(1)} %get-tuple-element.9), custom_call_target="InvertDiagBlocksLowerTriangular" | custom-call | tf_op jit(solution)/shard_map/jit(_solve_triangular)/triangular_solve | solution.py:31
  798.3 144.3 %all_gather.29 = f32[512,256]{1,0:T(8,128)S(1)} all-gather(f32[16,256]{1,0:T(8,128)S(1)} %fusion.7), channel_id=1, replica_groups=mesh['row'=16,'col'=32] {'col'}, dimensions={0}, use_global_device_ids=true | all-gather | bytes 540672 | tf_op jit(solution)/shard_map/all_gather | solution.py:61
  942.6 0.7 dynamic-slice_select_fusion.2
  943.3 107.1 %all-gather.11.cloned.1.call-done = f32[2048,256]{1,0:T(8,128)} async-done(((f32[128,256]{1,0:T(8,128)}), f32[2048,256]{1,0:T(8,128)}) %all-gather.11.cloned.1.call-update) | async-done | bytes 2097168 | tf_op jit(solution)/shard_map/all_gather | solution.py:13
  1050.4 1.7 reduce_sum.32
  1052.2 1.3 convolution_subtract_fusion
  (37 shorter events, 3.1 us)
Async XLA Ops:
  7.2 154.3 %all-gather.7.cloned.1.call-start = ((), (), s32[]{:S(2)}) async-start(), calls=%async_computation.2 | async-start | bytes 13369344 | tf_op jit(solution)/shard_map/all_gather | solution.py:13
  10.2 443.6 %reduce-scatter.2.cloned.1.call-start = ((), (), s32[]{:S(2)}) async-start(), calls=%async_computation.1 | async-start | bytes 540672 | tf_op jit(solution)/shard_map/reduce_scatter | solution.py:46
  161.4 6.9 copy-start
  169.7 565.3 %all-gather.9.cloned.1.call-start = ((), (), s32[]{:S(2)}) async-start(), calls=%async_computation.3 | async-start | bytes 4456448 | tf_op jit(solution)/shard_map/all_gather | solution.py:13
  591.0 459.4 %all-gather.11.cloned.1.call-start = ((), (), s32[]{:S(2)}) async-start(), calls=%async_computation.4 | async-start | bytes 2228224 | tf_op jit(solution)/shard_map/all_gather | solution.py:13
  798.3 253.8 %copy-start.2 = (f32[16,256]{1,0:T(8,128)}, f32[16,256]{1,0:T(8,128)S(1)}, u32[]{:S(2)}) copy-start(f32[16,256]{1,0:T(8,128)S(1)} %fusion.7) | copy-start | bytes 49156
  798.3 253.8 %copy-start.1 = (f32[512,128]{1,0:T(8,128)S(1)}, f32[512,128]{1,0:T(8,128)}, u32[]{:S(2)}) copy-start(f32[512,128]{1,0:T(8,128)} %param.5) | copy-start | bytes 786436
Sparse Core Ops, SparseCore 0:
  10.3 151.0 all-gather.6
  169.9 283.9 reduce-scatter.1
  591.1 143.8 all-gather.8
  943.4 106.9 all-gather.10
